TPU v7x, 32 devices: a whole 2x2x4 slice. The times are simulated.
32 devices in a mesh: section: 2 (over core), dp: 8 (over z, y), cls: 2 (over x).
Axes of the slice: x: 2, y: 2, z: 4, core: 2. Of those that a mesh axis runs over, the one named last changes fastest.
Arguments:
- embeddings: bfloat16 [1024, 512], P('dp')
- centers: bfloat16 [131072, 512], P(('section', 'dp', 'cls'))
- sample_ids: int32 [32, 1536], P(('section', 'dp', 'cls')), may hold values from 0 to 4095, as said below
- labels: int32 [1024], P('dp'), may hold values from 0 to 131071, as said below
Outputs:
- feature_grad: float32 [1024, 512], P(('section', 'dp', 'cls'))
- row_loss: float32 [1024], P('dp')
Inputs may be any that keep to these rules, and one draw needn't show every extreme that they name: `sample_ids`: the 1536 entries of each row are distinct. For each row, labels // 4096 names a shard j, and labels % 4096 is among sample_ids[j].
All inputs are finite; a program needn't handle non-finite values.
Results may differ from a plain program's by a relative error of at most 0.0033.
Values may be sent and summed in bfloat16 or wider, within the bound.
A program may use at most 64 MiB of HBM per device.

v0:
```python
import jax
import jax.numpy as jnp
from jax import lax
from jax.sharding import PartitionSpec as P

LOGIT_SCALE = 64.0
MARGIN = 0.35
EPSILON = 1e-06


def on_device(embeddings, centers, sample_ids, labels):
    shard_index = lax.axis_index(("section", "dp", "cls"))
    per_shard = centers.shape[0]
    gathered, label_all = (
        lax.all_gather(embeddings, "dp", axis=0, tiled=True),
        lax.all_gather(labels, "dp", axis=0, tiled=True),
    )
    total_rows = gathered.shape[0]
    emb_float = gathered.astype(jnp.float32)
    row_norm = jnp.sqrt(jnp.sum(emb_float * emb_float, axis=1) + EPSILON)
    unit_rows = (emb_float / row_norm[:, None]).astype(jnp.bfloat16)
    local_ids = sample_ids[0]
    chosen = jnp.take(centers, local_ids, axis=0).astype(jnp.float32)
    center_norm = jnp.sqrt(jnp.sum(chosen * chosen, axis=1) + EPSILON)
    unit_centers = (chosen / center_norm[:, None]).astype(jnp.bfloat16)
    cosine = lax.dot_general(
        unit_rows, unit_centers, (((1,), (1,)), ((), ())), preferred_element_type=jnp.float32
    )
    local_labels = label_all - shard_index * per_shard
    matches = local_ids[None, :] == local_labels[:, None]
    logits = LOGIT_SCALE * cosine - LOGIT_SCALE * MARGIN * matches.astype(jnp.float32)
    exponent = jnp.exp(logits)
    total_part = jnp.sum(exponent, axis=1)
    target_part = jnp.sum(jnp.where(matches, logits, jnp.float32(0.0)), axis=1)
    total, target = lax.psum((total_part, target_part), ("section", "dp", "cls"))
    weights = exponent.astype(jnp.bfloat16)
    column_ids = jnp.arange(local_ids.shape[0], dtype=jnp.int32)
    position = jnp.sum(jnp.where(matches, column_ids[None, :], 0), axis=1)
    owned = jnp.any(matches, axis=1).astype(jnp.float32)
    own_center = jnp.take(unit_centers, position, axis=0).astype(jnp.float32) * owned[:, None]
    section_count = lax.axis_size("section")
    batch_count = lax.axis_size("dp")
    class_count = lax.axis_size("cls")
    rows_here = total_rows // (section_count * batch_count * class_count)
    unscaled = jnp.dot(weights, unit_centers, preferred_element_type=jnp.float32)
    unit_grad = lax.psum_scatter(
        LOGIT_SCALE * (unscaled / total[:, None] - own_center),
        ("section", "dp", "cls"),
        scatter_dimension=0,
        tiled=True,
    )
    emb_rows = lax.dynamic_slice_in_dim(emb_float, shard_index * rows_here, rows_here, 0)
    norm_rows = lax.dynamic_slice_in_dim(row_norm, shard_index * rows_here, rows_here, 0)
    unit_float = emb_rows / norm_rows[:, None]
    along = jnp.sum(unit_float * unit_grad, axis=1, keepdims=True)
    feature_grad = (unit_grad - unit_float * along) / norm_rows[:, None]
    loss_all = jnp.log(total) - target
    own_rows = embeddings.shape[0]
    row_loss = lax.dynamic_slice_in_dim(loss_all, lax.axis_index("dp") * own_rows, own_rows, 0)
    return (feature_grad, row_loss)


def solution(mesh):
    return jax.shard_map(
        on_device,
        mesh=mesh,
        in_specs=(
            P("dp", None),
            P(("section", "dp", "cls"), None),
            P(("section", "dp", "cls"), None),
            P("dp"),
        ),
        out_specs=(P(("section", "dp", "cls"), None), P("dp")),
        check_vma=False,
    )
```

profile of v0, /device:TPU:0, one launch (start us, length us, event | category | flops | bytes accessed | tf_op | source)
XLA Modules:
  0.0 257.9 jit_solution(6422534031622051914)
XLA Ops:
  7.2 0.0 all-gather.3.cloned.1.call-start
  7.2 0.7 all-gather.3.cloned.1.call-update
  7.9 0.0 reduce-scatter.2.cloned.1.call-start
  7.9 0.7 fusion.8
  8.7 0.7 reduce
  9.4 22.3 %all-gather = s32[8,1,128]{2,1,0:T(1,128)S(1)} all-gather(s32[1,1,128]{2,1,0:T(1,128)} %bitcast.16), channel_id=1, replica_groups=mesh['section'=2,'dp'=8,'cls'=2] {'dp'}, dimensions={0}, use_global_device_ids=true | all-gather | bytes 4608 | tf_op jit(solution)/shard_map/all_gather | solution.py:16
  31.7 1.0 fusion.1
  32.7 0.9 compare_reduce_fusion
  33.7 7.6 %gather_fusion = bf16[1536,512]{1,0:T(8,128)(2,1)S(1)} fusion(bf16[4096,512]{1,0:T(8,128)(2,1)} %param.5, s32[2048]{0:T(1024)S(1)} %pad_clamp_fusion), kind=kCustom, calls=%fused_computation | custom fusion | bytes 3151872 | tf_op jit(solution)/shard_map/jit(_take)/gather | solution.py:23
  41.3 0.8 fusion.3
  42.1 1.1 fusion.4
  43.2 4.0 %gather_fusion.1 = bf16[1024,512]{1,0:T(8,128)(2,1)S(1)} fusion(bf16[1536,512]{1,0:T(8,128)(2,1)S(1)} %fusion.4, s32[1024]{0:T(1024)S(1)} %broadcast_clamp_fusion), kind=kCustom, calls=%fused_computation.1 | custom fusion | bytes 2101248 | tf_op jit(solution)/shard_map/jit(_take)/gather | solution.py:40
  47.2 5.9 %all-gather.3.cloned.1.call-done = bf16[1024,512]{1,0:T(8,128)(2,1)} async-done(((bf16[128,512]{1,0:T(8,128)(2,1)}), bf16[1024,512]{1,0:T(8,128)(2,1)}) %all-gather.3.cloned.1.call-update) | async-done | bytes 1048592 | tf_op jit(solution)/shard_map/all_gather | solution.py:15
  53.1 1.5 multiply_reduce_fusion
  54.6 6.4 %fusion.2 = (f32[1024]{0:T(1024)S(1)}, f32[1024]{0:T(1024)S(1)}, f32[1024,1536]{1,0:T(8,128)}) fusion(s32[1536]{0:T(1024)S(1)} %reduce, s32[1024]{0:T(1024)S(1)} %bitcast.13, bf16[1536,512]{1,0:T(8,128)(2,1)S(1)} %fusion.4, f32[1024]{0:T(1024)S(1)} %add_sqrt_fusion.1, bf16[1024,512]{1,0:T(8,128)(2,1)} %all-gather.3.cloned.1.call-done), kind=kOutput, calls=%fused_computation.8 | convolution fusion | flops 1623193600 | bytes 8935424 | tf_op jit(solution)/shard_map/dot_general | solution.py:26
  61.0 38.3 %all-reduce = (f32[1024]{0:T(1024)S(1)}, f32[1024]{0:T(1024)S(1)}) all-reduce(f32[1024]{0:T(1024)S(1)} %get-tuple-element.3, f32[1024]{0:T(1024)S(1)} %get-tuple-element.2), channel_id=1, replica_groups=mesh['section'=2,'dp'=8,'cls'=2] {'section','dp','cls'}, use_global_device_ids=true, to_apply=%region_3.4 | all-reduce | flops 2048 | bytes 16384 | tf_op jit(solution)/shard_map/psum | solution.py:35
  99.3 6.0 %subtract_multiply_fusion = f32[1024,512]{1,0:T(8,128)} fusion(bf16[1536,512]{1,0:T(8,128)(2,1)S(1)} %fusion.4, f32[1024,1536]{1,0:T(8,128)} %get-tuple-element.6, f32[1024]{0:T(1024)S(1)} %convert_element_type.32, bf16[1024,512]{1,0:T(8,128)(2,1)S(1)} %gather_fusion.1, f32[1024]{0:T(1024)S(1)} %get-tuple-element.4, pred[1024]{0:T(1024)(128)(4,1)S(1)} %compare_and_fusion.1), kind=kOutput, calls=%fused_computation.16 | convolution fusion | flops 1615331328 | bytes 11019264 | tf_op jit(solution)/shard_map/dot_general | solution.py:45
  105.3 0.0 copy-start
  105.3 0.0 reduce-scatter.2.cloned.1.call-update
  105.4 0.1 dynamic_slice.10
  105.5 0.6 dynamic_slice.11
  106.0 0.5 copy-done
  106.6 0.3 convert_element_type.26
  106.9 141.7 %reduce-scatter.2.cloned.1.call-done = f32[32,512]{1,0:T(8,128)} async-done(((f32[1024,512]{1,0:T(8,128)}), f32[32,512]{1,0:T(8,128)}) %reduce-scatter.2.cloned.1.call-update) | async-done | bytes 65552 | tf_op jit(solution)/shard_map/reduce_scatter | solution.py:46
  248.5 1.0 multiply_reduce_fusion.1
  249.5 1.6 subtract_divide_fusion
  (10 shorter events, 0.1 us)
Async XLA Ops:
  7.2 45.9 %all-gather.3.cloned.1.call-start = ((), (), s32[]{:S(2)}) async-start(), calls=%async_computation.1 | async-start | bytes 1179648 | tf_op jit(solution)/shard_map/all_gather | solution.py:15
  7.9 240.6 %reduce-scatter.2.cloned.1.call-start = ((), (), s32[]{:S(2)}) async-start(), calls=%async_computation.2 | async-start | bytes 2162688 | tf_op jit(solution)/shard_map/reduce_scatter | solution.py:46
  105.3 1.2 copy-start
Sparse Core Ops, SparseCore 0:
  10.1 42.9 all-gather.2
  105.5 142.9 reduce-scatter.1
where the time goes:
time: 258 us
  waiting for transfers between devices  148 us (57%)
  blocking collectives  60.6 us (23%)
  between operations  14.2 us (6%)
  local copies, waits for them, and re-layouts  12.7 us (5%)
  matrix products  12.5 us (5%)
  other arithmetic  9.66 us (4%)
    reduce_scatter x1, waiting for transfers between devices, on_device(): lax.psum_scatter(LOGIT_SCALE * (unscaled / total[:, None] - own_center),...  142 us
    psum x1, blocking collectives, on_device(): lax.psum((total_part, target_part), ('section', 'dp', 'cls'))  38.3 us
    all_gather x1, blocking collectives, on_device(): lax.all_gather(labels, 'dp', axis=0, tiled=True)  22.3 us
    gather x1, local copies, waits for them, and re-layouts, on_device(): chosen = jnp.take(centers, local_ids, axis=0).astype(jnp.float32)  7.59 us
    dot_general x1, matrix products, on_device(): lax.dot_general(unit_rows, unit_centers, (((1,), (1,)), ((), ())), prefer...  6.42 us
    dot_general x1, matrix products, on_device(): jnp.dot(weights, unit_centers, preferred_element_type=jnp.float32)  6.05 us
    all_gather x1, waiting for transfers between devices, on_device(): lax.all_gather(embeddings, 'dp', axis=0, tiled=True)  5.86 us
  transfers between devices with their start and end apart: 2, of which 2 were waited for; matrix products, arithmetic and copies ran while one was open for 7% of the time, Pallas kernels for 0%

commit v1 on v0

v1 whole, which is shorter than its diff:
```python
import functools

import jax
import jax.numpy as jnp
from jax import lax
from jax.experimental import pallas as pl
from jax.experimental.pallas import tpu as pltpu
from jax.sharding import PartitionSpec as P

LOGIT_SCALE = 64.0
MARGIN = 0.35
EPSILON = 1e-06
LANES = 128
PICK_STEPS = 8
CHUNKS = 4
MESH = pl.DeviceIdType.MESH


def to_column(row):
    return jnp.transpose(jnp.broadcast_to(row, (LANES, LANES)))


def to_row(column):
    return jnp.transpose(jnp.broadcast_to(column, (LANES, LANES)))[:1, :]


def kernel(
    n_dp, n_cls,
    emb_ref, centers_hbm, ids_ref, labels_ref,
    grad_ref, loss_ref,
    centers, gathered, labels, ids_column, unit_centers, weights, onehot,
    sums, group_sums, all_sums,
    unscaled, own, unscaled_in, own_in, inverse,
    cls_out, cls_in, kept, dp_out, dp_in,
    centers_sem,
    dp_send, dp_recv, label_send, label_recv, cls_send, cls_recv, sec_send, sec_recv,
    group_send, group_recv, all_send, all_recv, half_send, half_recv,
    rows_send, rows_recv, piece_send, piece_recv,
):
    sec, dp, cls = lax.axis_index("section"), lax.axis_index("dp"), lax.axis_index("cls")
    n_group = 2 * n_cls
    group = sec * n_cls + cls
    shard = (sec * n_dp + dp) * n_cls + cls
    other = 1 - sec
    n_pieces, rh, width = emb_ref.shape
    per_shard = centers_hbm.shape[0]
    k_total = ids_ref.shape[1]
    half_pieces = n_dp * n_cls
    pieces_per_unit = 2 * n_pieces
    rows_per_unit = 2 * LANES

    def dp_peer(k):
        return lax.rem(dp + k, n_dp)

    def dp_source(k):
        return lax.rem(dp + n_dp - k, n_dp)

    def cls_peer(j):
        return lax.rem(cls + j, n_cls)

    def group_peer(j):
        g = lax.rem(group + j, n_group)
        return (g // n_cls, dp, lax.rem(g, n_cls))

    def remote(src, dst, send, recv, device):
        return pltpu.make_async_remote_copy(
            src_ref=src, dst_ref=dst, send_sem=send, recv_sem=recv,
            device_id=device, device_id_type=MESH,
        )

    load = pltpu.make_async_copy(centers_hbm, centers, centers_sem)
    load.start()

    barrier = pltpu.get_barrier_semaphore()
    for k in range(1, n_dp):
        pl.semaphore_signal(barrier, inc=1, device_id=(sec, dp_peer(k), cls), device_id_type=MESH)
    for j in range(1, n_group):
        pl.semaphore_signal(barrier, inc=1, device_id=group_peer(j), device_id_type=MESH)

    gathered[dp] = emb_ref[...]
    labels[dp] = labels_ref[...]
    ids_float = ids_ref[...].astype(jnp.float32)
    for i in range(k_total // LANES):
        ids_column[i * LANES:(i + 1) * LANES, :] = to_column(ids_float[:, i * LANES:(i + 1) * LANES])

    pl.semaphore_wait(barrier, n_dp - 1 + n_group - 1)

    def block_copy(k):
        return remote(
            emb_ref.at[group], gathered.at[dp, group], dp_send.at[k], dp_recv.at[k], (sec, dp_peer(k), cls)
        )

    def block_arrival(k):
        there = gathered.at[dp_source(k), group]
        return remote(there, there, dp_send.at[k], dp_recv.at[k], (sec, dp_peer(k), cls))

    def label_copy(k):
        return remote(labels_ref, labels.at[dp], label_send.at[k], label_recv.at[k], (sec, dp_peer(k), cls))

    def label_arrival(k):
        there = labels.at[dp_source(k)]
        return remote(there, there, label_send.at[k], label_recv.at[k], (sec, dp_peer(k), cls))

    def cls_copy(k, j):
        piece = gathered.at[dp_source(k), group]
        return remote(piece, piece, cls_send.at[j, k], cls_recv.at[j, k], (sec, dp, cls_peer(j)))

    def cls_arrival(k, j):
        piece = gathered.at[dp_source(k), sec * n_cls + lax.rem(cls + n_cls - j, n_cls)]
        return remote(piece, piece, cls_send.at[j, k], cls_recv.at[j, k], (sec, dp, cls_peer(j)))

    def sec_copy(k, owner):
        pieces = gathered.at[dp_source(k), pl.ds(owner * n_cls, n_cls)]
        return remote(pieces, pieces, sec_send.at[k], sec_recv.at[k], (other, dp, cls))

    for k in range(1, n_dp):
        block_copy(k).start()
    for k in range(1, n_dp):
        label_copy(k).start()

    def pass_to_cls(k):
        block_arrival(k).wait_recv()
        for j in range(1, n_cls):
            cls_copy(k, j).start()

    def pass_to_sec(k):
        for j in range(1, n_cls):
            cls_arrival(k, j).wait_recv()
        sec_copy(k, sec).start()

    load.wait()
    step_rows = k_total // PICK_STEPS
    per_step = n_dp // PICK_STEPS
    lag = 2 * per_step

    def pick(t, carry):
        for i in range(per_step):
            k = t * per_step + i

            @pl.when(k >= 1)
            def _():
                pass_to_cls(k)

            @pl.when(k - lag >= 1)
            def _():
                pass_to_sec(k - lag)

        start = pl.multiple_of(t * step_rows, step_rows)
        wanted = ids_column[pl.ds(start, step_rows), :]
        lane = lax.broadcasted_iota(jnp.int32, (step_rows, LANES), 1).astype(jnp.float32)
        pieces = []
        for i in range(per_shard // LANES):
            hit = wanted == lane + jnp.float32(i * LANES)
            pieces.append(jnp.where(hit, jnp.float32(1.0), jnp.float32(0.0)).astype(jnp.bfloat16))
        chosen = jnp.dot(jnp.concatenate(pieces, axis=1), centers[...], preferred_element_type=jnp.float32)
        norm = jnp.sqrt(jnp.sum(chosen * chosen, axis=1, keepdims=True) + EPSILON)
        unit_centers[pl.ds(start, step_rows), :] = (chosen * (1.0 / norm)).astype(jnp.bfloat16)
        return carry

    lax.fori_loop(0, PICK_STEPS, pick, 0)
    for k in range(n_dp - lag, n_dp):
        pass_to_sec(k)
    for k in range(1, n_dp):
        label_arrival(k).wait_recv()
    for k in range(1, n_dp):
        sec_copy(k, other).wait_recv()

    def score(u, carry):
        rows = gathered[pl.ds(2 * u, 2)].astype(jnp.float32).reshape(rows_per_unit, width)
        norm = jnp.sqrt(jnp.sum(rows * rows, axis=1, keepdims=True) + EPSILON)
        unit_rows = (rows * (1.0 / norm)).astype(jnp.bfloat16)
        local = []
        for i in range(2):
            local.append(to_column((labels[2 * u + i] - shard * per_shard).astype(jnp.float32)))
        local = jnp.concatenate(local, axis=0)
        cosine = lax.dot_general(
            unit_rows, unit_centers[...], (((1,), (1,)), ((), ())), preferred_element_type=jnp.float32
        )
        start = pl.multiple_of(u * rows_per_unit, rows_per_unit)
        total = jnp.zeros((rows_per_unit, LANES), jnp.float32)
        target = jnp.zeros((rows_per_unit, LANES), jnp.float32)
        for i in range(k_total // LANES):
            columns = slice(i * LANES, (i + 1) * LANES)
            matches = local == ids_ref[:, columns].astype(jnp.float32)
            logits = LOGIT_SCALE * cosine[:, columns]
            logits = jnp.where(matches, logits - LOGIT_SCALE * MARGIN, logits)
            exponent = jnp.exp(logits)
            total = total + exponent
            target = target + jnp.where(matches, logits, jnp.float32(0.0))
            weights[pl.ds(start, rows_per_unit), columns] = exponent.astype(jnp.bfloat16)
            onehot[pl.ds(start, rows_per_unit), columns] = jnp.where(
                matches, jnp.float32(1.0), jnp.float32(0.0)
            ).astype(jnp.bfloat16)
        total = jnp.sum(total, axis=1, keepdims=True)
        target = jnp.sum(target, axis=1, keepdims=True)
        for i in range(2):
            part = slice(i * LANES, (i + 1) * LANES)
            sums[2 * u + i] = jnp.concatenate([to_row(total[part]), to_row(target[part])], axis=0)
        return carry

    lax.fori_loop(0, n_dp // 2, score, 0)

    group_sums[group] = sums[...]

    def group_copy(j):
        return remote(sums, group_sums.at[group], group_send.at[j], group_recv.at[j], group_peer(j))

    def group_arrival(j):
        there = group_sums.at[lax.rem(group + n_group - j, n_group)]
        return remote(there, there, group_send.at[j], group_recv.at[j], group_peer(j))

    def all_copy(k):
        return remote(
            all_sums.at[dp], all_sums.at[dp], all_send.at[k], all_recv.at[k], (sec, dp_peer(k), cls)
        )

    def all_arrival(k):
        there = all_sums.at[dp_source(k)]
        return remote(there, there, all_send.at[k], all_recv.at[k], (sec, dp_peer(k), cls))

    for j in range(1, n_group):
        group_copy(j).start()

    units_per_half = n_dp // 4

    def weigh_half(half):
        def weigh(i, carry):
            u = half * units_per_half + i
            start = pl.multiple_of(u * rows_per_unit, rows_per_unit)
            dst = pl.ds(i * pieces_per_unit, pieces_per_unit)
            shape = (pieces_per_unit, rh, width)
            unscaled[half, dst] = jnp.dot(
                weights[pl.ds(start, rows_per_unit), :], unit_centers[...], preferred_element_type=jnp.float32
            ).reshape(shape)
            own[half, dst] = jnp.dot(
                onehot[pl.ds(start, rows_per_unit), :], unit_centers[...], preferred_element_type=jnp.float32
            ).reshape(shape).astype(jnp.bfloat16)
            return carry

        lax.fori_loop(0, units_per_half, weigh, 0)

    weigh_half(other)
    half_copies = [
        remote(unscaled.at[other], unscaled_in, half_send.at[0], half_recv.at[0], (other, dp, cls)),
        remote(own.at[other], own_in, half_send.at[1], half_recv.at[1], (other, dp, cls)),
    ]
    for copy in half_copies:
        copy.start()

    for j in range(1, n_group):
        group_arrival(j).wait_recv()
    group_total = group_sums[0]
    for j in range(1, n_group):
        group_total = group_total + group_sums[j]
    all_sums[dp] = group_total
    for k in range(1, n_dp):
        all_copy(k).start()

    weigh_half(sec)

    for k in range(1, n_dp):
        all_arrival(k).wait_recv()
    sums_all = all_sums[0]
    for k in range(1, n_dp):
        sums_all = sums_all + all_sums[k]
    group_sums[group] = sums_all
    mine = group_sums[group, dp]
    loss_ref[...] = jnp.log(mine[:1, :]) - mine[1:, :]
    for b in range(n_dp // 2):
        block = group_sums[group, sec * (n_dp // 2) + b]
        inverse[b * n_pieces:(b + 1) * n_pieces] = to_column(LOGIT_SCALE / block[:1, :]).reshape(
            n_pieces, rh, LANES
        )
    for copy in half_copies:
        copy.wait_recv()

    def gradient(k, column):
        p = dp_peer(k) * n_cls + column
        scale = jnp.concatenate([inverse[p]] * (width // LANES), axis=1)
        centers_here = own[sec, p].astype(jnp.float32) + own_in[p].astype(jnp.float32)
        return (unscaled[sec, p] + unscaled_in[p]) * scale - LOGIT_SCALE * centers_here

    per_chunk = n_dp // CHUNKS

    def rows_copy(j, q):
        part = pl.ds(q * per_chunk, per_chunk)
        return remote(
            cls_out.at[j, part], cls_in.at[j, part], rows_send.at[j, q], rows_recv.at[j, q], (sec, dp, cls_peer(j))
        )

    def piece_copy(k):
        return remote(dp_out.at[k], dp_in.at[k], piece_send.at[k], piece_recv.at[k], (sec, dp_peer(k), cls))

    order = list(range(CHUNKS))[::-1]
    for q in order:
        for j in range(1, n_cls):
            for k in range(q * per_chunk, (q + 1) * per_chunk):
                cls_out[j, k] = gradient(k, cls_peer(j)).astype(jnp.bfloat16)
            rows_copy(j, q).start()
    for k in range(n_dp):
        kept[k] = gradient(k, cls)
    for q in order:
        for j in range(1, n_cls):
            rows_copy(j, q).wait_recv()
        for k in range(q * per_chunk, (q + 1) * per_chunk):
            value = kept[k]
            for j in range(1, n_cls):
                value = value + cls_in[j, k].astype(jnp.float32)
            if k == 0:
                kept[0] = value
            else:
                dp_out[k] = value.astype(jnp.bfloat16)
                piece_copy(k).start()

    rows = gathered[shard // n_group, lax.rem(shard, n_group)].astype(jnp.float32)
    norm = jnp.sqrt(jnp.sum(rows * rows, axis=1, keepdims=True) + EPSILON)
    inverse_norm = 1.0 / norm
    unit_rows = rows * inverse_norm
    unit_grad = kept[0]
    for k in list(range(1, n_dp))[::-1]:
        piece_copy(k).wait_recv()
        unit_grad = unit_grad + dp_in[k].astype(jnp.float32)
    along = jnp.sum(unit_rows * unit_grad, axis=1, keepdims=True)
    grad_ref[...] = (unit_grad - unit_rows * along) * inverse_norm

    for k in range(1, n_dp):
        block_copy(k).wait_send()
        label_copy(k).wait_send()
        sec_copy(k, sec).wait_send()
        all_copy(k).wait_send()
        piece_copy(k).wait_send()
        for j in range(1, n_cls):
            cls_copy(k, j).wait_send()
    for j in range(1, n_group):
        group_copy(j).wait_send()
    for copy in half_copies:
        copy.wait_send()
    for j in range(1, n_cls):
        for q in range(CHUNKS):
            rows_copy(j, q).wait_send()


def on_device(n_dp, n_cls, embeddings, centers, sample_ids, labels):
    block_rows, width = embeddings.shape
    n_pieces = 2 * n_cls
    rh = block_rows // n_pieces
    k_total = sample_ids.shape[1]
    rows = block_rows * n_dp
    half_pieces = n_dp * n_cls
    f32, bf16 = jnp.float32, jnp.bfloat16
    dma = pltpu.SemaphoreType.DMA
    vmem = pl.BlockSpec(memory_space=pltpu.VMEM)
    grad, loss = pl.pallas_call(
        functools.partial(kernel, n_dp, n_cls),
        out_shape=(
            jax.ShapeDtypeStruct((rh, width), f32),
            jax.ShapeDtypeStruct((1, block_rows), f32),
        ),
        in_specs=[vmem, pl.BlockSpec(memory_space=pl.ANY), vmem, vmem],
        out_specs=(vmem, vmem),
        scratch_shapes=[
            pltpu.VMEM(centers.shape, bf16),
            pltpu.VMEM((n_dp, n_pieces, rh, width), bf16),
            pltpu.VMEM((n_dp, 1, block_rows), jnp.int32),
            pltpu.VMEM((k_total, LANES), f32),
            pltpu.VMEM((k_total, width), bf16),
            pltpu.VMEM((rows, k_total), bf16),
            pltpu.VMEM((rows, k_total), bf16),
            pltpu.VMEM((n_dp, 2, block_rows), f32),
            pltpu.VMEM((n_pieces, n_dp, 2, block_rows), f32),
            pltpu.VMEM((n_dp, n_dp, 2, block_rows), f32),
            pltpu.VMEM((2, half_pieces, rh, width), f32),
            pltpu.VMEM((2, half_pieces, rh, width), bf16),
            pltpu.VMEM((half_pieces, rh, width), f32),
            pltpu.VMEM((half_pieces, rh, width), bf16),
            pltpu.VMEM((half_pieces, rh, LANES), f32),
            pltpu.VMEM((n_cls, n_dp, rh, width), bf16),
            pltpu.VMEM((n_cls, n_dp, rh, width), bf16),
            pltpu.VMEM((n_dp, rh, width), f32),
            pltpu.VMEM((n_dp, rh, width), bf16),
            pltpu.VMEM((n_dp, rh, width), bf16),
            dma,
            dma((n_dp,)), dma((n_dp,)), dma((n_dp,)), dma((n_dp,)),
            dma((n_cls, n_dp)), dma((n_cls, n_dp)), dma((n_dp,)), dma((n_dp,)),
            dma((n_pieces,)), dma((n_pieces,)), dma((n_dp,)), dma((n_dp,)),
            dma((2,)), dma((2,)),
            dma((n_cls, CHUNKS)), dma((n_cls, CHUNKS)), dma((n_dp,)), dma((n_dp,)),
        ],
        compiler_params=pltpu.CompilerParams(
            collective_id=0, has_side_effects=True, vmem_limit_bytes=52 * 1024 * 1024
        ),
    )(embeddings.reshape(n_pieces, rh, width), centers, sample_ids, labels.reshape(1, block_rows))
    return grad, loss.reshape(block_rows)


def solution(mesh):
    n_dp, n_cls = mesh.shape["dp"], mesh.shape["cls"]
    return jax.shard_map(
        functools.partial(on_device, n_dp, n_cls),
        mesh=mesh,
        in_specs=(
            P("dp", None),
            P(("section", "dp", "cls"), None),
            P(("section", "dp", "cls"), None),
            P("dp"),
        ),
        out_specs=(P(("section", "dp", "cls"), None), P("dp")),
        check_vma=False,
    )
```

time: 258 us -> 51 us (0.20)
  waiting for transfers between devices: 148 us -> 0 us
  blocking collectives: 60.6 us -> 0 us
  Pallas kernels: 0 us -> 46.7 us
  between operations: 14.2 us -> 0.65 us
  matrix products: 12.5 us -> 0 us
  other arithmetic: 9.66 us -> 0 us
  local copies, waits for them, and re-layouts: 12.7 us -> 3.39 us
    reduce_scatter x1 -> x0, waiting for transfers between devices: 142 us -> none  [on_device(): lax.psum_scatter(LOGIT_SCALE * (unscaled / total[:, None] - own_center),...]
    pallas_call x0 -> x1, Pallas kernels: none -> 46.7 us  [on_device(): pl.pallas_call(functools.partial(kernel, n_dp, n_cls), out_shape=(jax.Sha...]
    psum x1 -> x0, blocking collectives: 38.3 us -> none  [on_device(): lax.psum((total_part, target_part), ('section', 'dp', 'cls'))]
    all_gather x1 -> x0, blocking collectives: 22.3 us -> none  [on_device(): lax.all_gather(labels, 'dp', axis=0, tiled=True)]
    dot_general x2 -> x0, matrix products: 12.5 us -> none  [the longest x1 6.42 us: on_device(): lax.dot_general(unit_rows, unit_centers, (((1,), (1,)), ((), ())), prefer...]
    gather x2 -> x0, local copies, waits for them, and re-layouts: 11.6 us -> none  [the longest x1 7.59 us: on_device(): chosen = jnp.take(centers, local_ids, axis=0).astype(jnp.float32)]
    all_gather x1 -> x0, waiting for transfers between devices: 5.86 us -> none  [on_device(): lax.all_gather(embeddings, 'dp', axis=0, tiled=True)]
    reduce_sum x4 -> x0, other arithmetic: 4.28 us -> none  [the longest x1 1.5 us: on_device(): row_norm = jnp.sqrt(jnp.sum(emb_float * emb_float, axis=1) + EPSILON)]
  transfers between devices with their start and end apart: 2 -> 0, of which waited for: 2 -> 0; matrix products, arithmetic and copies ran while one was open for 7% -> 0% of each run, Pallas kernels for 0% -> 0%
where the time goes in v1:
time: 51 us; the launch traced here: 50.8 us
  Pallas kernels  46.7 us (92%)
  local copies, waits for them, and re-layouts  3.39 us (7%)
  between operations  0.65 us (1%)
    pallas_call x1, Pallas kernels, on_device(): pl.pallas_call(functools.partial(kernel, n_dp, n_cls), out_shape=(jax.Sha...  46.7 us
    unnamed x8, local copies, waits for them, and re-layouts  3.39 us

profile of v1, /device:TPU:0, one launch (start us, length us, event | category | flops | bytes accessed | tf_op | source)
XLA Modules:
  0.0 50.8 jit_solution(13926295864660428098)
XLA Ops:
  0.6 0.0 copy-start
  0.6 0.9 %copy-done = bf16[128,512]{1,0:T(8,128)(2,1)S(1)} copy-done((bf16[128,512]{1,0:T(8,128)(2,1)S(1)}, bf16[128,512]{1,0:T(8,128)(2,1)}, u32[]{:S(2)}) %copy-start) | copy-done | bytes 131096
  1.5 0.0 copy-start.1
  1.5 0.7 %copy-done.1 = s32[1,1536]{1,0:T(1,128)S(1)} copy-done((s32[1,1536]{1,0:T(1,128)S(1)}, s32[1,1536]{1,0:T(1,128)}, u32[]{:S(2)}) %copy-start.1) | copy-done | bytes 6168
  2.2 0.0 copy-start.2
  2.2 0.7 %copy-done.2 = s32[128]{0:T(128)S(1)} copy-done((s32[128]{0:T(128)S(1)}, s32[128]{0:T(128)}, u32[]{:S(2)}) %copy-start.2) | copy-done | bytes 536
  2.9 46.7 %shard_map.59 = (f32[32,512]{1,0:T(8,128)S(1)}, f32[1,128]{1,0:T(1,128)S(1)}) custom-call(bf16[4,32,512]{2,1,0:T(8,128)(2,1)S(1)} %bitcast.3, bf16[4096,512]{1,0:T(8,128)(2,1)} %centers_hbm.1, s32[1,1536]{1,0:T(1,128)S(1)} %copy-done.1, s32[1,128]{1,0:T(1,128)S(1)} %bitcast.4), custom_call_target="tpu_custom_call" | custom-call | tf_op jit(solution)/shard_map/pallas_call | solution.py:353
  49.6 0.6 %copy.8 = f32[32,512]{1,0:T(8,128)} copy(f32[32,512]{1,0:T(8,128)S(1)} %get-tuple-element.8) | data formatting | bytes 131072
  50.2 0.5 %copy.9 = f32[128]{0:T(128)} copy(f32[128]{0:T(128)S(1)} %bitcast.5) | data formatting | bytes 1024
Async XLA Ops:
  0.6 0.9 %copy-start = (bf16[128,512]{1,0:T(8,128)(2,1)S(1)}, bf16[128,512]{1,0:T(8,128)(2,1)}, u32[]{:S(2)}) copy-start(bf16[128,512]{1,0:T(8,128)(2,1)} %param.4) | copy-start | bytes 393220
  1.5 0.7 %copy-start.1 = (s32[1,1536]{1,0:T(1,128)S(1)}, s32[1,1536]{1,0:T(1,128)}, u32[]{:S(2)}) copy-start(s32[1,1536]{1,0:T(1,128)} %ids_ref.1) | copy-start | bytes 18436
  2.2 0.7 %copy-start.2 = (s32[128]{0:T(128)S(1)}, s32[128]{0:T(128)}, u32[]{:S(2)}) copy-start(s32[128]{0:T(128)} %param.7) | copy-start | bytes 1540

commit v2 on v1

--- a/solution.py
+++ b/solution.py
@@ -11,7 +11,8 @@
 MARGIN = 0.35
 EPSILON = 1e-06
 LANES = 128
-PICK_STEPS = 8
+PICK_STEPS = 4
+UNIT = 4
 CHUNKS = 4
 MESH = pl.DeviceIdType.MESH
 
@@ -26,13 +27,13 @@
 
 def kernel(
     n_dp, n_cls,
-    emb_ref, centers_hbm, ids_ref, labels_ref,
+    emb_hbm, centers_hbm, ids_hbm, labels_hbm,
     grad_ref, loss_ref,
-    centers, gathered, labels, ids_column, unit_centers, weights, onehot,
+    centers, gathered, labels, ids_ref, ids_column, unit_centers, weights, onehot,
     sums, group_sums, all_sums,
     unscaled, own, unscaled_in, own_in, inverse,
     cls_out, cls_in, kept, dp_out, dp_in,
-    centers_sem,
+    centers_sem, inputs_sem,
     dp_send, dp_recv, label_send, label_recv, cls_send, cls_recv, sec_send, sec_recv,
     group_send, group_recv, all_send, all_recv, half_send, half_recv,
     rows_send, rows_recv, piece_send, piece_recv,
@@ -42,12 +43,12 @@
     group = sec * n_cls + cls
     shard = (sec * n_dp + dp) * n_cls + cls
     other = 1 - sec
-    n_pieces, rh, width = emb_ref.shape
+    n_pieces, rh, width = emb_hbm.shape
     per_shard = centers_hbm.shape[0]
-    k_total = ids_ref.shape[1]
+    k_total = ids_hbm.shape[1]
     half_pieces = n_dp * n_cls
-    pieces_per_unit = 2 * n_pieces
-    rows_per_unit = 2 * LANES
+    pieces_per_unit = UNIT * n_pieces
+    rows_per_unit = UNIT * LANES
 
     def dp_peer(k):
         return lax.rem(dp + k, n_dp)
@@ -69,6 +70,13 @@
         )
 
     load = pltpu.make_async_copy(centers_hbm, centers, centers_sem)
+    inputs = [
+        pltpu.make_async_copy(ids_hbm, ids_ref, inputs_sem.at[0]),
+        pltpu.make_async_copy(emb_hbm, gathered.at[dp], inputs_sem.at[1]),
+        pltpu.make_async_copy(labels_hbm, labels.at[dp], inputs_sem.at[2]),
+    ]
+    for copy in inputs:
+        copy.start()
     load.start()
 
     barrier = pltpu.get_barrier_semaphore()
@@ -77,8 +85,8 @@
     for j in range(1, n_group):
         pl.semaphore_signal(barrier, inc=1, device_id=group_peer(j), device_id_type=MESH)
 
-    gathered[dp] = emb_ref[...]
-    labels[dp] = labels_ref[...]
+    for copy in inputs:
+        copy.wait()
     ids_float = ids_ref[...].astype(jnp.float32)
     for i in range(k_total // LANES):
         ids_column[i * LANES:(i + 1) * LANES, :] = to_column(ids_float[:, i * LANES:(i + 1) * LANES])
@@ -87,7 +95,7 @@
 
     def block_copy(k):
         return remote(
-            emb_ref.at[group], gathered.at[dp, group], dp_send.at[k], dp_recv.at[k], (sec, dp_peer(k), cls)
+            gathered.at[dp, group], gathered.at[dp, group], dp_send.at[k], dp_recv.at[k], (sec, dp_peer(k), cls)
         )
 
     def block_arrival(k):
@@ -95,7 +103,7 @@
         return remote(there, there, dp_send.at[k], dp_recv.at[k], (sec, dp_peer(k), cls))
 
     def label_copy(k):
-        return remote(labels_ref, labels.at[dp], label_send.at[k], label_recv.at[k], (sec, dp_peer(k), cls))
+        return remote(labels.at[dp], labels.at[dp], label_send.at[k], label_recv.at[k], (sec, dp_peer(k), cls))
 
     def label_arrival(k):
         there = labels.at[dp_source(k)]
@@ -131,7 +139,7 @@
     load.wait()
     step_rows = k_total // PICK_STEPS
     per_step = n_dp // PICK_STEPS
-    lag = 2 * per_step
+    lag = per_step
 
     def pick(t, carry):
         for i in range(per_step):
@@ -166,12 +174,12 @@
         sec_copy(k, other).wait_recv()
 
     def score(u, carry):
-        rows = gathered[pl.ds(2 * u, 2)].astype(jnp.float32).reshape(rows_per_unit, width)
+        rows = gathered[pl.ds(UNIT * u, UNIT)].astype(jnp.float32).reshape(rows_per_unit, width)
         norm = jnp.sqrt(jnp.sum(rows * rows, axis=1, keepdims=True) + EPSILON)
         unit_rows = (rows * (1.0 / norm)).astype(jnp.bfloat16)
         local = []
-        for i in range(2):
-            local.append(to_column((labels[2 * u + i] - shard * per_shard).astype(jnp.float32)))
+        for i in range(UNIT):
+            local.append(to_column((labels[UNIT * u + i] - shard * per_shard).astype(jnp.float32)))
         local = jnp.concatenate(local, axis=0)
         cosine = lax.dot_general(
             unit_rows, unit_centers[...], (((1,), (1,)), ((), ())), preferred_element_type=jnp.float32
@@ -193,12 +201,12 @@
             ).astype(jnp.bfloat16)
         total = jnp.sum(total, axis=1, keepdims=True)
         target = jnp.sum(target, axis=1, keepdims=True)
-        for i in range(2):
+        for i in range(UNIT):
             part = slice(i * LANES, (i + 1) * LANES)
-            sums[2 * u + i] = jnp.concatenate([to_row(total[part]), to_row(target[part])], axis=0)
+            sums[UNIT * u + i] = jnp.concatenate([to_row(total[part]), to_row(target[part])], axis=0)
         return carry
 
-    lax.fori_loop(0, n_dp // 2, score, 0)
+    lax.fori_loop(0, n_dp // UNIT, score, 0)
 
     group_sums[group] = sums[...]
 
@@ -221,7 +229,7 @@
     for j in range(1, n_group):
         group_copy(j).start()
 
-    units_per_half = n_dp // 4
+    units_per_half = n_dp // (2 * UNIT)
 
     def weigh_half(half):
         def weigh(i, carry):
@@ -356,12 +364,13 @@
             jax.ShapeDtypeStruct((rh, width), f32),
             jax.ShapeDtypeStruct((1, block_rows), f32),
         ),
-        in_specs=[vmem, pl.BlockSpec(memory_space=pl.ANY), vmem, vmem],
+        in_specs=[pl.BlockSpec(memory_space=pltpu.HBM)] * 4,
         out_specs=(vmem, vmem),
         scratch_shapes=[
             pltpu.VMEM(centers.shape, bf16),
             pltpu.VMEM((n_dp, n_pieces, rh, width), bf16),
             pltpu.VMEM((n_dp, 1, block_rows), jnp.int32),
+            pltpu.VMEM((1, k_total), jnp.int32),
             pltpu.VMEM((k_total, LANES), f32),
             pltpu.VMEM((k_total, width), bf16),
             pltpu.VMEM((rows, k_total), bf16),
@@ -379,7 +388,7 @@
             pltpu.VMEM((n_dp, rh, width), f32),
             pltpu.VMEM((n_dp, rh, width), bf16),
             pltpu.VMEM((n_dp, rh, width), bf16),
-            dma,
+            dma, dma((3,)),
             dma((n_dp,)), dma((n_dp,)), dma((n_dp,)), dma((n_dp,)),
             dma((n_cls, n_dp)), dma((n_cls, n_dp)), dma((n_dp,)), dma((n_dp,)),
             dma((n_pieces,)), dma((n_pieces,)), dma((n_dp,)), dma((n_dp,)),

time: 51 us -> 49.9 us (0.978)
  Pallas kernels: 46.7 us -> 45.6 us
    pallas_call x1, Pallas kernels: 46.7 us -> 45.6 us  [on_device(): pl.pallas_call(functools.partial(kernel, n_dp, n_cls), out_shape=(jax.Sha...]
where the time goes in v2:
time: 49.9 us; the launch traced here: 49.7 us
  Pallas kernels  45.6 us (91%)
  local copies, waits for them, and re-layouts  3.39 us (7%)
  between operations  0.65 us (1%)
    pallas_call x1, Pallas kernels, on_device(): pl.pallas_call(functools.partial(kernel, n_dp, n_cls), out_shape=(jax.Sha...  45.6 us
    unnamed x8, local copies, waits for them, and re-layouts  3.39 us

profile of v2, /device:TPU:0, one launch (start us, length us, event | category | flops | bytes accessed | tf_op | source)
XLA Modules:
  0.0 49.7 jit_solution(1880511347309823581)
XLA Ops:
  0.6 0.0 copy-start
  0.6 0.9 %copy-done = bf16[128,512]{1,0:T(8,128)(2,1)S(1)} copy-done((bf16[128,512]{1,0:T(8,128)(2,1)S(1)}, bf16[128,512]{1,0:T(8,128)(2,1)}, u32[]{:S(2)}) %copy-start) | copy-done | bytes 131096
  1.5 0.0 copy-start.1
  1.5 0.7 %copy-done.1 = s32[1,1536]{1,0:T(1,128)S(1)} copy-done((s32[1,1536]{1,0:T(1,128)S(1)}, s32[1,1536]{1,0:T(1,128)}, u32[]{:S(2)}) %copy-start.1) | copy-done | bytes 6168
  2.2 0.0 copy-start.2
  2.2 0.7 %copy-done.2 = s32[128]{0:T(128)S(1)} copy-done((s32[128]{0:T(128)S(1)}, s32[128]{0:T(128)}, u32[]{:S(2)}) %copy-start.2) | copy-done | bytes 536
  2.9 45.6 %shard_map.59 = (f32[32,512]{1,0:T(8,128)S(1)}, f32[1,128]{1,0:T(1,128)S(1)}) custom-call(bf16[4,32,512]{2,1,0:T(8,128)(2,1)S(1)} %bitcast.3, bf16[4096,512]{1,0:T(8,128)(2,1)} %centers_hbm.1, s32[1,1536]{1,0:T(1,128)S(1)} %copy-done.1, s32[1,128]{1,0:T(1,128)S(1)} %bitcast.4), custom_call_target="tpu_custom_call" | custom-call | tf_op jit(solution)/shard_map/pallas_call | solution.py:361
  48.5 0.6 %copy.8 = f32[32,512]{1,0:T(8,128)} copy(f32[32,512]{1,0:T(8,128)S(1)} %get-tuple-element.8) | data formatting | bytes 131072
  49.2 0.5 %copy.9 = f32[128]{0:T(128)} copy(f32[128]{0:T(128)S(1)} %bitcast.5) | data formatting | bytes 1024
Async XLA Ops:
  0.6 0.9 %copy-start = (bf16[128,512]{1,0:T(8,128)(2,1)S(1)}, bf16[128,512]{1,0:T(8,128)(2,1)}, u32[]{:S(2)}) copy-start(bf16[128,512]{1,0:T(8,128)(2,1)} %param.4) | copy-start | bytes 393220
  1.5 0.7 %copy-start.1 = (s32[1,1536]{1,0:T(1,128)S(1)}, s32[1,1536]{1,0:T(1,128)}, u32[]{:S(2)}) copy-start(s32[1,1536]{1,0:T(1,128)} %ids_hbm.1) | copy-start | bytes 18436
  2.2 0.7 %copy-start.2 = (s32[128]{0:T(128)S(1)}, s32[128]{0:T(128)}, u32[]{:S(2)}) copy-start(s32[128]{0:T(128)} %param.7) | copy-start | bytes 1540

commit v3 on v2

--- a/solution.py
+++ b/solution.py
@@ -139,19 +139,27 @@
     load.wait()
     step_rows = k_total // PICK_STEPS
     per_step = n_dp // PICK_STEPS
-    lag = per_step
 
     def pick(t, carry):
         for i in range(per_step):
             k = t * per_step + i
 
-            @pl.when(k >= 1)
+            @pl.when(t >= 1)
             def _():
                 pass_to_cls(k)
 
-            @pl.when(k - lag >= 1)
+            @pl.when(t >= 2)
             def _():
-                pass_to_sec(k - lag)
+                pass_to_sec(k - per_step)
+
+        for k in range(1, per_step):
+            @pl.when(t == 1)
+            def _():
+                pass_to_cls(k)
+
+            @pl.when(t == 2)
+            def _():
+                pass_to_sec(k)
 
         start = pl.multiple_of(t * step_rows, step_rows)
         wanted = ids_column[pl.ds(start, step_rows), :]
@@ -166,25 +174,32 @@
         return carry
 
     lax.fori_loop(0, PICK_STEPS, pick, 0)
-    for k in range(n_dp - lag, n_dp):
+    for k in range(n_dp - per_step, n_dp):
         pass_to_sec(k)
     for k in range(1, n_dp):
         label_arrival(k).wait_recv()
-    for k in range(1, n_dp):
-        sec_copy(k, other).wait_recv()
 
     def score(u, carry):
-        rows = gathered[pl.ds(UNIT * u, UNIT)].astype(jnp.float32).reshape(rows_per_unit, width)
+        for i in range(UNIT):
+            k = UNIT * u + i
+
+            @pl.when(k >= 1)
+            def _():
+                sec_copy(k, other).wait_recv()
+
+        blocks = [dp_source(UNIT * u + i) for i in range(UNIT)]
+        starts = [pl.multiple_of(b * LANES, LANES) for b in blocks]
+        rows = [gathered[b].reshape(LANES, width) for b in blocks]
+        rows = jnp.concatenate(rows, axis=0).astype(jnp.float32)
         norm = jnp.sqrt(jnp.sum(rows * rows, axis=1, keepdims=True) + EPSILON)
         unit_rows = (rows * (1.0 / norm)).astype(jnp.bfloat16)
         local = []
         for i in range(UNIT):
-            local.append(to_column((labels[UNIT * u + i] - shard * per_shard).astype(jnp.float32)))
+            local.append(to_column((labels[blocks[i]] - shard * per_shard).astype(jnp.float32)))
         local = jnp.concatenate(local, axis=0)
         cosine = lax.dot_general(
             unit_rows, unit_centers[...], (((1,), (1,)), ((), ())), preferred_element_type=jnp.float32
         )
-        start = pl.multiple_of(u * rows_per_unit, rows_per_unit)
         total = jnp.zeros((rows_per_unit, LANES), jnp.float32)
         target = jnp.zeros((rows_per_unit, LANES), jnp.float32)
         for i in range(k_total // LANES):
@@ -195,15 +210,16 @@
             exponent = jnp.exp(logits)
             total = total + exponent
             target = target + jnp.where(matches, logits, jnp.float32(0.0))
-            weights[pl.ds(start, rows_per_unit), columns] = exponent.astype(jnp.bfloat16)
-            onehot[pl.ds(start, rows_per_unit), columns] = jnp.where(
-                matches, jnp.float32(1.0), jnp.float32(0.0)
-            ).astype(jnp.bfloat16)
+            exponent = exponent.astype(jnp.bfloat16)
+            hits = jnp.where(matches, jnp.float32(1.0), jnp.float32(0.0)).astype(jnp.bfloat16)
+            for b in range(UNIT):
+                weights[pl.ds(starts[b], LANES), columns] = exponent[b * LANES:(b + 1) * LANES]
+                onehot[pl.ds(starts[b], LANES), columns] = hits[b * LANES:(b + 1) * LANES]
         total = jnp.sum(total, axis=1, keepdims=True)
         target = jnp.sum(target, axis=1, keepdims=True)
         for i in range(UNIT):
             part = slice(i * LANES, (i + 1) * LANES)
-            sums[UNIT * u + i] = jnp.concatenate([to_row(total[part]), to_row(target[part])], axis=0)
+            sums[blocks[i]] = jnp.concatenate([to_row(total[part]), to_row(target[part])], axis=0)
         return carry
 
     lax.fori_loop(0, n_dp // UNIT, score, 0)

time: 49.9 us -> 49.9 us (level)
  no operation moved by 1% of the time
where the time goes in v3:
time: 49.9 us; the launch traced here: 49.7 us
  Pallas kernels  45.7 us (92%)
  local copies, waits for them, and re-layouts  3.39 us (7%)
  between operations  0.65 us (1%)
    pallas_call x1, Pallas kernels, on_device(): pl.pallas_call(functools.partial(kernel, n_dp, n_cls), out_shape=(jax.Sha...  45.7 us
    unnamed x8, local copies, waits for them, and re-layouts  3.39 us

profile of v3, /device:TPU:0, one launch (start us, length us, event | category | flops | bytes accessed | tf_op | source)
XLA Modules:
  0.0 49.7 jit_solution(9589707648002718240)
XLA Ops:
  0.6 0.0 copy-start
  0.6 0.9 %copy-done = bf16[128,512]{1,0:T(8,128)(2,1)S(1)} copy-done((bf16[128,512]{1,0:T(8,128)(2,1)S(1)}, bf16[128,512]{1,0:T(8,128)(2,1)}, u32[]{:S(2)}) %copy-start) | copy-done | bytes 131096
  1.5 0.0 copy-start.1
  1.5 0.7 %copy-done.1 = s32[1,1536]{1,0:T(1,128)S(1)} copy-done((s32[1,1536]{1,0:T(1,128)S(1)}, s32[1,1536]{1,0:T(1,128)}, u32[]{:S(2)}) %copy-start.1) | copy-done | bytes 6168
  2.2 0.0 copy-start.2
  2.2 0.7 %copy-done.2 = s32[128]{0:T(128)S(1)} copy-done((s32[128]{0:T(128)S(1)}, s32[128]{0:T(128)}, u32[]{:S(2)}) %copy-start.2) | copy-done | bytes 536
  2.9 45.7 %shard_map.59 = (f32[32,512]{1,0:T(8,128)S(1)}, f32[1,128]{1,0:T(1,128)S(1)}) custom-call(bf16[4,32,512]{2,1,0:T(8,128)(2,1)S(1)} %bitcast.3, bf16[4096,512]{1,0:T(8,128)(2,1)} %centers_hbm.1, s32[1,1536]{1,0:T(1,128)S(1)} %copy-done.1, s32[1,128]{1,0:T(1,128)S(1)} %bitcast.4), custom_call_target="tpu_custom_call" | custom-call | tf_op jit(solution)/shard_map/pallas_call | solution.py:377
  48.6 0.6 %copy.8 = f32[32,512]{1,0:T(8,128)} copy(f32[32,512]{1,0:T(8,128)S(1)} %get-tuple-element.8) | data formatting | bytes 131072
  49.2 0.5 %copy.9 = f32[128]{0:T(128)} copy(f32[128]{0:T(128)S(1)} %bitcast.5) | data formatting | bytes 1024
Async XLA Ops:
  0.6 0.9 %copy-start = (bf16[128,512]{1,0:T(8,128)(2,1)S(1)}, bf16[128,512]{1,0:T(8,128)(2,1)}, u32[]{:S(2)}) copy-start(bf16[128,512]{1,0:T(8,128)(2,1)} %param.4) | copy-start | bytes 393220
  1.5 0.7 %copy-start.1 = (s32[1,1536]{1,0:T(1,128)S(1)}, s32[1,1536]{1,0:T(1,128)}, u32[]{:S(2)}) copy-start(s32[1,1536]{1,0:T(1,128)} %ids_hbm.1) | copy-start | bytes 18436
  2.2 0.7 %copy-start.2 = (s32[128]{0:T(128)S(1)}, s32[128]{0:T(128)}, u32[]{:S(2)}) copy-start(s32[128]{0:T(128)} %param.7) | copy-start | bytes 1540
